TPU v7x, 32 devices: a whole 2x2x4 slice. The times are simulated.
32 devices in a mesh: dp: 4 (over z), ctx: 8 (over y, x, core).
Axes of the slice: x: 2, y: 2, z: 4, core: 2. Of those that a mesh axis runs over, the one named last changes fastest.
Arguments:
- gate_in: bfloat16 [4, 2048, 2048], P('dp', 'ctx'), may hold values from -6 to 6
- values: bfloat16 [4, 2048, 2048], P('dp', 'ctx'), may hold values from -6 to 6
- gate_out: bfloat16 [4, 2048, 2048], P('dp', 'ctx'), may hold values from -6 to 6
- cotangent: bfloat16 [4, 2048, 2048], P('dp', 'ctx'), may hold values from -6 to 6
- filters: bfloat16 [2048, 2048], P(None, 'ctx'), may hold values from -6 to 6
- skip_gain: float32 [2048], replicated, may hold values from -3 to 3
Outputs:
- grad_gate_in: bfloat16 [4, 2048, 2048], P('dp', 'ctx')
- grad_values: bfloat16 [4, 2048, 2048], P('dp', 'ctx')
- grad_gate_out: bfloat16 [4, 2048, 2048], P('dp', 'ctx')
- grad_filters: float32 [2048, 2048], P('dp', 'ctx')
All inputs are finite; a program needn't handle non-finite values.
Results may differ from a plain program's by a relative error of at most 0.014.
Values may be sent and summed in bfloat16 or wider, within the bound.
A program may use at most 128 MiB of HBM per device.

v0:
```python
import functools
import math

import jax
import jax.numpy as jnp
import ml_dtypes
import numpy as np
from jax import lax
from jax.experimental import pallas as pl
from jax.experimental.pallas import tpu as pltpu
from jax.sharding import PartitionSpec as P

RADIX = 128
GROUP = 16
BF16 = jnp.bfloat16
F32 = jnp.float32


def make_tables(length):
    half = length // RADIX
    size = 2 * length
    scale = length ** (-0.5) / size
    groups = RADIX // GROUP
    a = np.arange(half)
    b = np.arange(RADIX)
    j = np.arange(half)
    pos = 128 * a[None, :] + b[:, None]
    ang = 2 * math.pi * ((pos[:, None, :] * j[None, :, None]) % size) / size
    first = np.stack([np.cos(ang), -np.sin(ang)], 2)
    first[:, 0, 0, :] = 1.0
    first[:, 0, 1, :] = (-1.0) ** a[None, :]
    last = first * np.where(j == 0, scale, 2 * scale)[None, :, None, None]
    first = first.reshape(groups, GROUP, half, 2, half)
    last = last.reshape(groups, GROUP, half, 2, half)
    eye = np.eye(GROUP)
    table_a = np.einsum("gijpa,ik->gjpiak", first, eye).reshape(
        groups, half * 2 * GROUP, half * GROUP
    )
    table_e = np.einsum("gijpa,ik->gaijpk", last, eye).reshape(
        groups, half * GROUP, half * 2 * GROUP
    )
    ang = 2 * math.pi * (np.outer(b, b) % RADIX) / RADIX
    cos, sin = np.cos(ang), np.sin(ang)
    general = np.block([[cos, sin], [-sin, cos]])
    inverse = np.block([[cos, -sin], [sin, cos]])
    hr = RADIX // 2
    packed = np.zeros((2, RADIX, 2, RADIX))
    packed_inv = np.zeros((2, RADIX, 2, RADIX))
    s = np.arange(hr)
    ang0 = 2 * math.pi * (np.outer(s, b) % RADIX) / RADIX
    packed[0, :hr, 0] = np.cos(ang0)
    packed[1, :hr, 0] = -np.sin(ang0)
    packed[1, 0, 0] = (-1.0) ** b
    ang1 = 2 * math.pi * (np.outer(2 * s + 1, b) % (2 * RADIX)) / (2 * RADIX)
    packed[0, hr:, 1] = np.cos(ang1)
    packed[1, hr:, 1] = -np.sin(ang1)
    packed_inv = 2.0 * np.transpose(packed, (2, 3, 0, 1))
    packed_inv[0, :, 0, 0] = 1.0
    packed_inv[0, :, 1, 0] = (-1.0) ** b
    full = 2 * RADIX
    table_b = np.stack([packed.reshape(full, full), general])
    table_c = np.stack([packed_inv.reshape(full, full), inverse])
    return tuple(t.astype(ml_dtypes.bfloat16) for t in (table_a, table_b, table_c, table_e))


def dot(left, right):
    return jnp.dot(left, right, preferred_element_type=F32)


def partner(me, step, count):
    if count & (count - 1):
        return lax.rem(me + step, count)
    peer = me
    bit = 1
    while bit < count:
        if step & bit:
            peer = peer + bit * (1 - 2 * ((me // bit) % 2))
        bit *= 2
    return peer


def send_order(count):
    return sorted(range(1, count), key=lambda k: (-(k // 2).bit_count(), k))


def spectral_product(left, right, conj_left, packed):
    lr = left[:RADIX].astype(F32)
    li = left[RADIX:].astype(F32)
    rr = right[:RADIX].astype(F32)
    ri = right[RADIX:].astype(F32)
    real_real = lr * rr
    imag_imag = li * ri
    if conj_left:
        real = real_real + imag_imag
        imag = lr * ri - li * rr
    else:
        real = real_real - imag_imag
        imag = lr * ri + li * rr
    if packed:
        first = lax.broadcasted_iota(jnp.int32, lr.shape, 0) == 0
        real = jnp.where(first, real_real, real)
        imag = jnp.where(first, imag_imag, imag)
    return jnp.concatenate([real, imag], 0).astype(BF16)


def kernel(
    n_ctx,
    n_dp,
    gin_h,
    val_h,
    gout_h,
    cot_h,
    filt_h,
    ta_h,
    tb_h,
    tc_h,
    te_h,
    conv_out,
    back_out,
    part_out,
    gin,
    val,
    gout,
    cot,
    filt,
    ta,
    tb,
    tc,
    te,
    gated,
    cgrad,
    gated_ch,
    cgrad_ch,
    mid,
    spec_f,
    spec_g,
    mixed,
    mixed_x,
    conv_ch,
    back_ch,
    own_ch,
    load_sem,
    own_sem,
    send_sem,
    recv_sem,
    dp_send,
    dp_recv,
):
    me = lax.axis_index("ctx")
    seq = lax.axis_index("dp")
    tok, _ = gin.shape
    length, chans = filt.shape
    half = length // RADIX
    groups = RADIX // GROUP
    piece = length // n_dp

    barrier = pltpu.get_barrier_semaphore()
    for k in range(1, n_ctx):
        pl.semaphore_signal(barrier, inc=1, device_id={"ctx": partner(me, k, n_ctx)})
    for k in range(1, n_dp):
        pl.semaphore_signal(barrier, inc=1, device_id={"dp": partner(seq, k, n_dp)})

    loads = []
    for i, (src, dst) in enumerate(
        [
            (gin_h, gin),
            (val_h, val),
            (cot_h, cot),
            (gout_h, gout),
            (filt_h, filt),
            (ta_h, ta),
            (tb_h, tb),
            (tc_h, tc),
            (te_h, te),
        ]
    ):
        copy = pltpu.make_async_copy(src, dst, load_sem.at[i])
        copy.start()
        loads.append(copy)

    def columns(index):
        return pl.ds(pl.multiple_of(index * chans, chans), chans)

    def rows(index, count):
        return pl.ds(pl.multiple_of(index * count, count), count)

    def forward_sends(which, left, right, staged, landed):
        copies = []
        for k in send_order(n_ctx):
            peer = partner(me, k, n_ctx)
            block = left[:, columns(peer)].astype(F32) * right[:, columns(peer)].astype(F32)
            staged[:, columns(peer)] = block.astype(BF16)
            copy = pltpu.make_async_remote_copy(
                src_ref=staged.at[:, columns(peer)],
                dst_ref=landed.at[rows(me, tok), :],
                send_sem=send_sem.at[which, k],
                recv_sem=recv_sem.at[which, k],
                device_id={"ctx": peer},
            )
            copy.start()
            copies.append(copy)
        block = left[:, columns(me)].astype(F32) * right[:, columns(me)].astype(F32)
        landed[rows(me, tok), :] = block.astype(BF16)
        return copies

    def return_sends(which, source, target):
        copies = []
        for k in send_order(n_ctx):
            peer = partner(me, k, n_ctx)
            copy = pltpu.make_async_remote_copy(
                src_ref=source.at[rows(peer, tok), :],
                dst_ref=target.at[:, columns(me)],
                send_sem=send_sem.at[which, k],
                recv_sem=recv_sem.at[which, k],
                device_id={"ctx": peer},
            )
            copy.start()
            copies.append(copy)
        own = pltpu.make_async_copy(
            source.at[rows(me, tok), :], target.at[:, columns(me)], own_sem.at[which - 2]
        )
        own.start()
        return copies, own

    def first_stage(source):
        def body(g, carry):
            part = [source[pl.ds(pl.multiple_of(a * RADIX + g * GROUP, GROUP), GROUP), :]
                    for a in range(half)]
            out = dot(ta[g], jnp.concatenate(part, 0)).astype(BF16)
            for row in range(2 * half):
                mid[pl.ds(pl.multiple_of(row * RADIX + g * GROUP, GROUP), GROUP), :] = out[
                    row * GROUP : (row + 1) * GROUP
                ]
            return carry

        lax.fori_loop(0, groups, body, 0)

    def last_stage(source, target):
        def body(g, carry):
            part = [source[pl.ds(pl.multiple_of(row * RADIX + g * GROUP, GROUP), GROUP), :]
                    for row in range(2 * half)]
            out = dot(te[g], jnp.concatenate(part, 0)).astype(BF16)
            for a in range(half):
                target[pl.ds(pl.multiple_of(a * RADIX + g * GROUP, GROUP), GROUP), :] = out[
                    a * GROUP : (a + 1) * GROUP
                ]
            return carry

        lax.fori_loop(0, groups, body, 0)

    def each_row(step):
        step(0, True)

        def body(j, carry):
            step(j, False)
            return carry

        lax.fori_loop(1, half, body, 0)

    def spectrum(j, packed):
        table = tb[0 if packed else 1]
        return dot(table, mid[rows(j, 2 * RADIX), :]).astype(BF16)

    def unmix(target, j, packed, product):
        table = tc[0 if packed else 1]
        target[rows(j, 2 * RADIX), :] = dot(table, product).astype(BF16)

    loads[0].wait()
    loads[1].wait()
    pl.semaphore_wait(barrier, n_ctx - 1 + n_dp - 1)
    sent_gated = forward_sends(0, gin, val, gated, gated_ch)
    loads[2].wait()
    loads[3].wait()
    sent_cgrad = forward_sends(1, cot, gout, cgrad, cgrad_ch)

    for copy in loads[4:]:
        copy.wait()
    first_stage(filt)

    def filter_row(j, packed):
        spec_f[rows(j, 2 * RADIX), :] = spectrum(j, packed)

    each_row(filter_row)

    for copy in sent_gated:
        copy.wait_recv()
    first_stage(gated_ch)

    def gated_row(j, packed):
        spec = spectrum(j, packed)
        spec_g[rows(j, 2 * RADIX), :] = spec
        unmix(mixed, j, packed, spectral_product(
            spec_f[rows(j, 2 * RADIX), :], spec, False, packed))

    each_row(gated_row)
    last_stage(mixed, conv_ch)
    sent_conv, own_conv = return_sends(2, conv_ch, conv_out)

    for copy in sent_cgrad:
        copy.wait_recv()
    first_stage(cgrad_ch)

    def cgrad_row(j, packed):
        spec = spectrum(j, packed)
        unmix(mixed_x, j, packed, spectral_product(
            spec_g[rows(j, 2 * RADIX), :], spec, True, packed))
        unmix(mixed, j, packed, spectral_product(
            spec_f[rows(j, 2 * RADIX), :], spec, True, packed))

    each_row(cgrad_row)
    last_stage(mixed_x, own_ch)
    sent_part = []
    for k in range(1, n_dp):
        peer = partner(seq, k, n_dp)
        copy = pltpu.make_async_remote_copy(
            src_ref=own_ch.at[rows(peer, piece), :],
            dst_ref=part_out.at[seq],
            send_sem=dp_send.at[k],
            recv_sem=dp_recv.at[k],
            device_id={"dp": peer},
        )
        copy.start()
        sent_part.append(copy)
    own_part = pltpu.make_async_copy(
        own_ch.at[rows(seq, piece), :], part_out.at[seq], own_sem.at[2]
    )
    own_part.start()
    last_stage(mixed, back_ch)
    sent_back, own_back = return_sends(3, back_ch, back_out)

    for copy in sent_gated + sent_cgrad:
        copy.wait_send()
    own_conv.wait()
    own_back.wait()
    own_part.wait()
    for copy in sent_conv + sent_back + sent_part:
        copy.wait()


def transfer_and_transform(gin, val, gout, cot, filters):
    n_ctx = lax.axis_size("ctx")
    n_dp = lax.axis_size("dp")
    tok, width = gin.shape
    length, chans = filters.shape
    tables = [jnp.asarray(t) for t in make_tables(length)]
    full = 2 * length
    any_spec = pl.BlockSpec(memory_space=pl.ANY)
    outs = (
        jax.ShapeDtypeStruct((tok, width), BF16),
        jax.ShapeDtypeStruct((tok, width), BF16),
        jax.ShapeDtypeStruct((n_dp, length // n_dp, chans), BF16),
    )
    vmem = lambda *shape: pltpu.VMEM(shape, BF16)
    dma = lambda *shape: pltpu.SemaphoreType.DMA(shape)
    return pl.pallas_call(
        functools.partial(kernel, n_ctx, n_dp),
        out_shape=outs,
        in_specs=[any_spec] * 9,
        out_specs=[any_spec] * 3,
        scratch_shapes=[vmem(tok, width)] * 4
        + [vmem(length, chans)]
        + [vmem(*t.shape) for t in tables]
        + [vmem(tok, width)] * 2
        + [vmem(length, chans)] * 2
        + [vmem(full, chans)] * 5
        + [vmem(length, chans)] * 3
        + [dma(9), dma(3), dma(4, n_ctx), dma(4, n_ctx), dma(n_dp), dma(n_dp)],
        compiler_params=pltpu.CompilerParams(
            collective_id=0, has_side_effects=True, vmem_limit_bytes=44 * 2**20
        ),
        cost_estimate=pl.CostEstimate(
            flops=12 * 2 * 512 * 256 * full * chans // 65536,
            bytes_accessed=12 * 2**20,
            transcendentals=0,
        ),
    )(gin, val, gout, cot, filters, *tables)


def on_device(gate_in, values, gate_out, cotangent, filters, skip_gain):
    conv, back, parts = transfer_and_transform(
        gate_in[0], values[0], gate_out[0], cotangent[0], filters
    )
    gin = gate_in[0].astype(F32)
    vals = values[0].astype(F32)
    cots = cotangent[0].astype(F32)
    gated = (gin * vals).astype(BF16).astype(F32)
    conv_grad = (cots * gate_out[0].astype(F32)).astype(BF16).astype(F32)
    gain = skip_gain[None, :]
    grad_gate_out = (cots * (conv.astype(F32) + gain * gated)).astype(BF16)
    grad_gated = back.astype(F32) + gain * conv_grad
    grad_gate_in = (grad_gated * vals).astype(BF16)
    grad_values = (grad_gated * gin).astype(BF16)
    grad_filters = jnp.sum(parts.astype(F32), axis=0)
    return (grad_gate_in[None], grad_values[None], grad_gate_out[None], grad_filters)


def solution(mesh):
    return jax.shard_map(
        on_device,
        mesh=mesh,
        in_specs=(
            P("dp", "ctx", None),
            P("dp", "ctx", None),
            P("dp", "ctx", None),
            P("dp", "ctx", None),
            P(None, "ctx"),
            P(),
        ),
        out_specs=(
            P("dp", "ctx", None),
            P("dp", "ctx", None),
            P("dp", "ctx", None),
            P("dp", "ctx"),
        ),
        check_vma=False,
    )
```

profile of v0, /device:TPU:9, one launch (start us, length us, event | category | flops | bytes accessed | tf_op | source)
XLA Modules:
  0.0 76.2 jit_solution(5536557550967727122)
XLA Ops:
  0.6 0.0 copy-start
  0.6 1.2 %copy-done = bf16[1,256,2048]{2,1,0:T(8,128)(2,1)S(1)} copy-done((bf16[1,256,2048]{2,1,0:T(8,128)(2,1)S(1)}, bf16[1,256,2048]{2,1,0:T(8,128)(2,1)}, u32[]{:S(2)}) %copy-start) | copy-done | bytes 1048600
  1.9 0.0 copy-start.1
  1.9 1.2 %copy-done.1 = bf16[1,256,2048]{2,1,0:T(8,128)(2,1)S(1)} copy-done((bf16[1,256,2048]{2,1,0:T(8,128)(2,1)S(1)}, bf16[1,256,2048]{2,1,0:T(8,128)(2,1)}, u32[]{:S(2)}) %copy-start.1) | copy-done | bytes 1048600
  3.1 0.0 copy-start.2
  3.1 1.2 %copy-done.2 = bf16[1,256,2048]{2,1,0:T(8,128)(2,1)S(1)} copy-done((bf16[1,256,2048]{2,1,0:T(8,128)(2,1)S(1)}, bf16[1,256,2048]{2,1,0:T(8,128)(2,1)}, u32[]{:S(2)}) %copy-start.2) | copy-done | bytes 1048600
  4.3 0.0 copy-start.3
  4.3 1.2 %copy-done.3 = bf16[1,256,2048]{2,1,0:T(8,128)(2,1)S(1)} copy-done((bf16[1,256,2048]{2,1,0:T(8,128)(2,1)S(1)}, bf16[1,256,2048]{2,1,0:T(8,128)(2,1)}, u32[]{:S(2)}) %copy-start.3) | copy-done | bytes 1048600
  5.5 0.0 copy-start.4
  5.5 1.2 %copy-done.4 = bf16[2048,256]{1,0:T(8,128)(2,1)S(1)} copy-done((bf16[2048,256]{1,0:T(8,128)(2,1)S(1)}, bf16[2048,256]{1,0:T(8,128)(2,1)}, u32[]{:S(2)}) %copy-start.4) | copy-done | bytes 1048600
  6.8 0.0 copy-start.5
  6.8 0.9 %copy-done.5 = bf16[2,256,256]{2,1,0:T(8,128)(2,1)S(1)} copy-done((bf16[2,256,256]{2,1,0:T(8,128)(2,1)S(1)}, bf16[2,256,256]{2,1,0:T(8,128)(2,1)}, u32[]{:S(2)}) %copy-start.5) | copy-done | bytes 262168
  7.7 0.0 copy-start.6
  7.7 0.9 %copy-done.6 = bf16[2,256,256]{2,1,0:T(8,128)(2,1)S(1)} copy-done((bf16[2,256,256]{2,1,0:T(8,128)(2,1)S(1)}, bf16[2,256,256]{2,1,0:T(8,128)(2,1)}, u32[]{:S(2)}) %copy-start.6) | copy-done | bytes 262168
  8.7 0.0 copy-start.7
  8.7 63.5 %shard_map.129 = (bf16[256,2048]{1,0:T(8,128)(2,1)S(1)}, bf16[256,2048]{1,0:T(8,128)(2,1)S(1)}, bf16[4,512,256]{2,1,0:T(8,128)(2,1)S(1)}) custom-call(bf16[256,2048]{1,0:T(8,128)(2,1)S(1)} %bitcast.19, bf16[256,2048]{1,0:T(8,128)(2,1)S(1)} %bitcast.20, bf16[256,2048]{1,0:T(8,128)(2,1)S(1)} %bitcast.21, bf16[256,2048]{1,0:T(8,128)(2,1)S(1)} %bitcast.22, ...), custom_call_target="tpu_custom_call" | custom-call | flops 50331648 | bytes 12582912 | tf_op jit(solution)/shard_map/pallas_call | solution.py:355
  72.2 0.9 %convert_reduce_fusion = f32[512,256]{1,0:T(8,128)} fusion(bf16[4,512,256]{2,1,0:T(8,128)(2,1)S(1)} %get-tuple-element.9), kind=kLoop, calls=%fused_computation.10 | loop fusion | flops 917504 | bytes 1572864 | tf_op jit(solution)/shard_map/reduce_sum | solution.py:393
  73.1 0.0 copy-done.7
  73.1 3.1 %fusion.5 = (bf16[1,256,2048]{2,1,0:T(8,128)(2,1)}, bf16[1,256,2048]{2,1,0:T(8,128)(2,1)}, bf16[1,256,2048]{2,1,0:T(8,128)(2,1)}) fusion(bf16[256,2048]{1,0:T(8,128)(2,1)S(1)} %get-tuple-element.7, f32[2048]{0:T(1024)S(1)} %copy-done.7, bf16[1,256,2048]{2,1,0:T(8,128)(2,1)S(1)} %copy-done.3, bf16[1,256,2048]{2,1,0:T(8,128)(2,1)S(1)} %copy-done.2, ...), kind=kLoop, calls=%fused_computation.12 | loop fusion | flops 11534336 | bytes 9445376 | tf_op jit(solution)/shard_map/broadcast_in_dim | solution.py:394
Async XLA Ops:
  0.6 1.2 %copy-start = (bf16[1,256,2048]{2,1,0:T(8,128)(2,1)S(1)}, bf16[1,256,2048]{2,1,0:T(8,128)(2,1)}, u32[]{:S(2)}) copy-start(bf16[1,256,2048]{2,1,0:T(8,128)(2,1)} %param.10) | copy-start | bytes 3145732
  1.9 1.2 %copy-start.1 = (bf16[1,256,2048]{2,1,0:T(8,128)(2,1)S(1)}, bf16[1,256,2048]{2,1,0:T(8,128)(2,1)}, u32[]{:S(2)}) copy-start(bf16[1,256,2048]{2,1,0:T(8,128)(2,1)} %param.11) | copy-start | bytes 3145732
  3.1 1.2 %copy-start.2 = (bf16[1,256,2048]{2,1,0:T(8,128)(2,1)S(1)}, bf16[1,256,2048]{2,1,0:T(8,128)(2,1)}, u32[]{:S(2)}) copy-start(bf16[1,256,2048]{2,1,0:T(8,128)(2,1)} %param.12) | copy-start | bytes 3145732
  4.3 1.2 %copy-start.3 = (bf16[1,256,2048]{2,1,0:T(8,128)(2,1)S(1)}, bf16[1,256,2048]{2,1,0:T(8,128)(2,1)}, u32[]{:S(2)}) copy-start(bf16[1,256,2048]{2,1,0:T(8,128)(2,1)} %param.13) | copy-start | bytes 3145732
  5.5 1.2 %copy-start.4 = (bf16[2048,256]{1,0:T(8,128)(2,1)S(1)}, bf16[2048,256]{1,0:T(8,128)(2,1)}, u32[]{:S(2)}) copy-start(bf16[2048,256]{1,0:T(8,128)(2,1)} %filt_h.1) | copy-start | bytes 3145732
  6.8 0.9 %copy-start.5 = (bf16[2,256,256]{2,1,0:T(8,128)(2,1)S(1)}, bf16[2,256,256]{2,1,0:T(8,128)(2,1)}, u32[]{:S(2)}) copy-start(bf16[2,256,256]{2,1,0:T(8,128)(2,1)} %constant.12.clone.tc_h) | copy-start | bytes 786436
  7.7 0.9 %copy-start.6 = (bf16[2,256,256]{2,1,0:T(8,128)(2,1)S(1)}, bf16[2,256,256]{2,1,0:T(8,128)(2,1)}, u32[]{:S(2)}) copy-start(bf16[2,256,256]{2,1,0:T(8,128)(2,1)} %constant.11.clone.tb_h) | copy-start | bytes 786436
  8.7 64.5 %copy-start.7 = (f32[2048]{0:T(1024)S(1)}, f32[2048]{0:T(1024)}, u32[]{:S(2)}) copy-start(f32[2048]{0:T(1024)} %param.15) | copy-start | bytes 24580
where the time goes:
time: 76.6 us; the launch traced here: 76.2 us
  Pallas kernels  63.5 us (83%)
  local copies, waits for them, and re-layouts  8.02 us (10%)
  other arithmetic  4.01 us (5%)
    pallas_call x1, Pallas kernels, transfer_and_transform(): pl.pallas_call(functools.partial(kernel, n_ctx, n_dp), out_shape=outs, in...  63.5 us
    unnamed x16, local copies, waits for them, and re-layouts  8.02 us
    broadcast_in_dim x1, other arithmetic, on_device(): grad_values[None]  3.07 us

commit v1 on v0

--- a/solution.py
+++ b/solution.py
@@ -127,32 +127,23 @@
     tb,
     tc,
     te,
-    gated,
-    cgrad,
-    gated_ch,
-    cgrad_ch,
     mid,
     spec_f,
-    spec_g,
     mixed,
     mixed_x,
-    conv_ch,
-    back_ch,
-    own_ch,
-    load_sem,
-    own_sem,
-    send_sem,
-    recv_sem,
-    dp_send,
-    dp_recv,
+    *rest,
 ):
     me = lax.axis_index("ctx")
     seq = lax.axis_index("dp")
     tok, _ = gin.shape
     length, chans = filt.shape
+    halves = max(1, chans // 128)
+    lanes = chans // halves
     half = length // RADIX
     groups = RADIX // GROUP
     piece = length // n_dp
+    staged, landed, ret, own = (rest[i * halves : (i + 1) * halves] for i in range(4))
+    load_sem, own_sem, send_sem, recv_sem, dp_send, dp_recv = rest[4 * halves :]
 
     barrier = pltpu.get_barrier_semaphore()
     for k in range(1, n_ctx):
@@ -178,162 +169,190 @@
         copy.start()
         loads.append(copy)
 
-    def columns(index):
-        return pl.ds(pl.multiple_of(index * chans, chans), chans)
+    def span(start, count, unit):
+        return pl.ds(pl.multiple_of(start, unit), count)
+
+    def pair(index):
+        return span(index * 2 * lanes, 2 * lanes, 2 * lanes)
 
     def rows(index, count):
-        return pl.ds(pl.multiple_of(index * count, count), count)
-
-    def forward_sends(which, left, right, staged, landed):
+        return span(index * count, count, count)
+
+    def gate(h, index, target, where):
+        cols = span(index * chans + h * lanes, lanes, lanes)
+        block = gin[:, cols].astype(F32) * val[:, cols].astype(F32)
+        grad = cot[:, cols].astype(F32) * gout[:, cols].astype(F32)
+        target[where] = jnp.concatenate([block, grad], 1).astype(BF16)
+
+    def forward_sends(h):
         copies = []
         for k in send_order(n_ctx):
             peer = partner(me, k, n_ctx)
-            block = left[:, columns(peer)].astype(F32) * right[:, columns(peer)].astype(F32)
-            staged[:, columns(peer)] = block.astype(BF16)
+            gate(h, peer, staged[h], (slice(None), pair(peer)))
             copy = pltpu.make_async_remote_copy(
-                src_ref=staged.at[:, columns(peer)],
-                dst_ref=landed.at[rows(me, tok), :],
-                send_sem=send_sem.at[which, k],
-                recv_sem=recv_sem.at[which, k],
+                src_ref=staged[h].at[:, pair(peer)],
+                dst_ref=landed[h].at[rows(me, tok), :],
+                send_sem=send_sem.at[h, k],
+                recv_sem=recv_sem.at[h, k],
                 device_id={"ctx": peer},
             )
             copy.start()
             copies.append(copy)
-        block = left[:, columns(me)].astype(F32) * right[:, columns(me)].astype(F32)
-        landed[rows(me, tok), :] = block.astype(BF16)
+        gate(h, me, landed[h], (rows(me, tok), slice(None)))
         return copies
 
-    def return_sends(which, source, target):
+    def return_sends(h):
         copies = []
-        for k in send_order(n_ctx):
-            peer = partner(me, k, n_ctx)
+        here = []
+        for t, target in enumerate((conv_out, back_out)):
+            dst = target.at[:, span(me * chans + h * lanes, lanes, lanes)]
+            cols = pl.ds(t * lanes, lanes)
+            for k in send_order(n_ctx):
+                peer = partner(me, k, n_ctx)
+                copy = pltpu.make_async_remote_copy(
+                    src_ref=ret[h].at[rows(peer, tok), cols],
+                    dst_ref=dst,
+                    send_sem=send_sem.at[halves + 2 * h + t, k],
+                    recv_sem=recv_sem.at[halves + 2 * h + t, k],
+                    device_id={"ctx": peer},
+                )
+                copy.start()
+                copies.append(copy)
+            copy = pltpu.make_async_copy(
+                ret[h].at[rows(me, tok), cols], dst, own_sem.at[2 * h + t]
+            )
+            copy.start()
+            here.append(copy)
+        return copies, here
+
+    def part_sends(h):
+        copies = []
+        cols = pl.ds(h * lanes, lanes)
+        for k in range(1, n_dp):
+            peer = partner(seq, k, n_dp)
             copy = pltpu.make_async_remote_copy(
-                src_ref=source.at[rows(peer, tok), :],
-                dst_ref=target.at[:, columns(me)],
-                send_sem=send_sem.at[which, k],
-                recv_sem=recv_sem.at[which, k],
-                device_id={"ctx": peer},
+                src_ref=own[h].at[rows(peer, piece), :],
+                dst_ref=part_out.at[seq, :, cols],
+                send_sem=dp_send.at[h, k],
+                recv_sem=dp_recv.at[h, k],
+                device_id={"dp": peer},
             )
             copy.start()
             copies.append(copy)
-        own = pltpu.make_async_copy(
-            source.at[rows(me, tok), :], target.at[:, columns(me)], own_sem.at[which - 2]
+        here = pltpu.make_async_copy(
+            own[h].at[rows(seq, piece), :], part_out.at[seq, :, cols], own_sem.at[2 * halves + h]
         )
-        own.start()
-        return copies, own
+        here.start()
+        return copies, [here]
+
+    def repeat(first, count, most, step):
+        width = max(w for w in range(1, most + 1) if count % w == 0)
+
+        def body(i, carry):
+            stores = [step(first + i * width + u) for u in range(width)]
+            for store in stores:
+                store()
+            return carry
+
+        lax.fori_loop(0, count // width, body, 0)
 
     def first_stage(source):
-        def body(g, carry):
-            part = [source[pl.ds(pl.multiple_of(a * RADIX + g * GROUP, GROUP), GROUP), :]
-                    for a in range(half)]
+        def step(g):
+            part = [source[span(a * RADIX + g * GROUP, GROUP, GROUP), :] for a in range(half)]
             out = dot(ta[g], jnp.concatenate(part, 0)).astype(BF16)
-            for row in range(2 * half):
-                mid[pl.ds(pl.multiple_of(row * RADIX + g * GROUP, GROUP), GROUP), :] = out[
-                    row * GROUP : (row + 1) * GROUP
-                ]
-            return carry
-
-        lax.fori_loop(0, groups, body, 0)
+
+            def store():
+                for row in range(2 * half):
+                    mid[span(row * RADIX + g * GROUP, GROUP, GROUP), : out.shape[1]] = out[
+                        row * GROUP : (row + 1) * GROUP
+                    ]
+
+            return store
+
+        repeat(0, groups, 4, step)
 
     def last_stage(source, target):
-        def body(g, carry):
-            part = [source[pl.ds(pl.multiple_of(row * RADIX + g * GROUP, GROUP), GROUP), :]
-                    for row in range(2 * half)]
+        def step(g):
+            part = [
+                source[span(row * RADIX + g * GROUP, GROUP, GROUP), :] for row in range(2 * half)
+            ]
             out = dot(te[g], jnp.concatenate(part, 0)).astype(BF16)
-            for a in range(half):
-                target[pl.ds(pl.multiple_of(a * RADIX + g * GROUP, GROUP), GROUP), :] = out[
-                    a * GROUP : (a + 1) * GROUP
-                ]
-            return carry
-
-        lax.fori_loop(0, groups, body, 0)
+
+            def store():
+                for a in range(half):
+                    target[span(a * RADIX + g * GROUP, GROUP, GROUP), :] = out[
+                        a * GROUP : (a + 1) * GROUP
+                    ]
+
+            return store
+
+        repeat(0, groups, 4, step)
+
+    def filter_row(j, packed):
+        where = rows(j, 2 * RADIX)
+        spec = dot(tb[0 if packed else 1], mid[where, :chans]).astype(BF16)
+
+        def store():
+            spec_f[where, :] = spec
+
+        return store
+
+    def half_row(h, j, packed):
+        where = rows(j, 2 * RADIX)
+        which = 0 if packed else 1
+        spec = dot(tb[which], mid[where, :]).astype(BF16)
+        spec_g, spec_c = spec[:, :lanes], spec[:, lanes:]
+        filt_row = spec_f[where, h * lanes : (h + 1) * lanes]
+        cross = spectral_product(spec_g, spec_c, True, packed)
+        both = jnp.concatenate(
+            [
+                spectral_product(filt_row, spec_g, False, packed),
+                spectral_product(filt_row, spec_c, True, packed),
+            ],
+            1,
+        )
+        out_x = dot(tc[which], cross).astype(BF16)
+        out = dot(tc[which], both).astype(BF16)
+
+        def store():
+            mixed_x[where, :] = out_x
+            mixed[where, :] = out
+
+        return store
 
     def each_row(step):
-        step(0, True)
-
-        def body(j, carry):
-            step(j, False)
-            return carry
-
-        lax.fori_loop(1, half, body, 0)
-
-    def spectrum(j, packed):
-        table = tb[0 if packed else 1]
-        return dot(table, mid[rows(j, 2 * RADIX), :]).astype(BF16)
-
-    def unmix(target, j, packed, product):
-        table = tc[0 if packed else 1]
-        target[rows(j, 2 * RADIX), :] = dot(table, product).astype(BF16)
-
-    loads[0].wait()
-    loads[1].wait()
+        step(0, True)()
+        repeat(1, half - 1, 5, lambda j: step(j, False))
+
+    for copy in loads[:4]:
+        copy.wait()
     pl.semaphore_wait(barrier, n_ctx - 1 + n_dp - 1)
-    sent_gated = forward_sends(0, gin, val, gated, gated_ch)
-    loads[2].wait()
-    loads[3].wait()
-    sent_cgrad = forward_sends(1, cot, gout, cgrad, cgrad_ch)
+    sent = [forward_sends(h) for h in range(halves)]
 
     for copy in loads[4:]:
         copy.wait()
     first_stage(filt)
-
-    def filter_row(j, packed):
-        spec_f[rows(j, 2 * RADIX), :] = spectrum(j, packed)
-
     each_row(filter_row)
 
-    for copy in sent_gated:
-        copy.wait_recv()
-    first_stage(gated_ch)
-
-    def gated_row(j, packed):
-        spec = spectrum(j, packed)
-        spec_g[rows(j, 2 * RADIX), :] = spec
-        unmix(mixed, j, packed, spectral_product(
-            spec_f[rows(j, 2 * RADIX), :], spec, False, packed))
-
-    each_row(gated_row)
-    last_stage(mixed, conv_ch)
-    sent_conv, own_conv = return_sends(2, conv_ch, conv_out)
-
-    for copy in sent_cgrad:
-        copy.wait_recv()
-    first_stage(cgrad_ch)
-
-    def cgrad_row(j, packed):
-        spec = spectrum(j, packed)
-        unmix(mixed_x, j, packed, spectral_product(
-            spec_g[rows(j, 2 * RADIX), :], spec, True, packed))
-        unmix(mixed, j, packed, spectral_product(
-            spec_f[rows(j, 2 * RADIX), :], spec, True, packed))
-
-    each_row(cgrad_row)
-    last_stage(mixed_x, own_ch)
-    sent_part = []
-    for k in range(1, n_dp):
-        peer = partner(seq, k, n_dp)
-        copy = pltpu.make_async_remote_copy(
-            src_ref=own_ch.at[rows(peer, piece), :],
-            dst_ref=part_out.at[seq],
-            send_sem=dp_send.at[k],
-            recv_sem=dp_recv.at[k],
-            device_id={"dp": peer},
-        )
-        copy.start()
-        sent_part.append(copy)
-    own_part = pltpu.make_async_copy(
-        own_ch.at[rows(seq, piece), :], part_out.at[seq], own_sem.at[2]
-    )
-    own_part.start()
-    last_stage(mixed, back_ch)
-    sent_back, own_back = return_sends(3, back_ch, back_out)
-
-    for copy in sent_gated + sent_cgrad:
+    remote = []
+    local = []
+    for h in range(halves):
+        for copy in sent[h]:
+            copy.wait_recv()
+        first_stage(landed[h])
+        each_row(functools.partial(half_row, h))
+        last_stage(mixed_x, own[h])
+        copies, here = part_sends(h)
+        remote += copies
+        local += here
+        last_stage(mixed, ret[h])
+        copies, here = return_sends(h)
+        remote += copies
+        local += here
+
+    for copy in sum(sent, []):
         copy.wait_send()
-    own_conv.wait()
-    own_back.wait()
-    own_part.wait()
-    for copy in sent_conv + sent_back + sent_part:
+    for copy in local + remote:
         copy.wait()
 
 
@@ -344,7 +363,9 @@
     length, chans = filters.shape
     tables = [jnp.asarray(t) for t in make_tables(length)]
     full = 2 * length
-    any_spec = pl.BlockSpec(memory_space=pl.ANY)
+    halves = max(1, chans // 128)
+    lanes = chans // halves
+    pair = 2 * lanes
     outs = (
         jax.ShapeDtypeStruct((tok, width), BF16),
         jax.ShapeDtypeStruct((tok, width), BF16),
@@ -355,18 +376,20 @@
     return pl.pallas_call(
         functools.partial(kernel, n_ctx, n_dp),
         out_shape=outs,
-        in_specs=[any_spec] * 9,
-        out_specs=[any_spec] * 3,
+        in_specs=[pl.BlockSpec(memory_space=pltpu.HBM)] * 9,
+        out_specs=[pl.BlockSpec(memory_space=pl.ANY)] * 3,
         scratch_shapes=[vmem(tok, width)] * 4
         + [vmem(length, chans)]
         + [vmem(*t.shape) for t in tables]
-        + [vmem(tok, width)] * 2
-        + [vmem(length, chans)] * 2
-        + [vmem(full, chans)] * 5
-        + [vmem(length, chans)] * 3
-        + [dma(9), dma(3), dma(4, n_ctx), dma(4, n_ctx), dma(n_dp), dma(n_dp)],
+        + [vmem(full, pair), vmem(full, chans), vmem(full, pair), vmem(full, lanes)]
+        + [vmem(tok, n_ctx * pair)] * halves
+        + [vmem(length, pair)] * halves
+        + [vmem(length, pair)] * halves
+        + [vmem(length, lanes)] * halves
+        + [dma(9), dma(3 * halves), dma(3 * halves, n_ctx), dma(3 * halves, n_ctx)]
+        + [dma(halves, n_dp), dma(halves, n_dp)],
         compiler_params=pltpu.CompilerParams(
-            collective_id=0, has_side_effects=True, vmem_limit_bytes=44 * 2**20
+            collective_id=0, has_side_effects=True, vmem_limit_bytes=56 * 2**20
         ),
         cost_estimate=pl.CostEstimate(
             flops=12 * 2 * 512 * 256 * full * chans // 65536,

time: 76.6 us -> 61.1 us (0.80)
  the two profiles are of different devices: /device:TPU:9 before, /device:TPU:0 now
where the time goes in v1:
time: 61.1 us; the launch traced here: 61 us
  Pallas kernels  53.3 us (87%)
  other arithmetic  6.93 us (11%)
  between operations  0.69 us (1%)
    pallas_call x1, Pallas kernels, transfer_and_transform(): pl.pallas_call(functools.partial(kernel, n_ctx, n_dp), out_shape=outs, in...  53.3 us
    broadcast_in_dim x1, other arithmetic, on_device(): grad_values[None]  4.64 us
    reduce_sum x1, other arithmetic, on_device(): grad_filters = jnp.sum(parts.astype(F32), axis=0)  2.29 us

profile of v1, /device:TPU:0, one launch (start us, length us, event | category | flops | bytes accessed | tf_op | source)
XLA Modules:
  0.0 61.0 jit_solution(8390018294634561473)
XLA Ops:
  0.6 0.0 copy-start.1
  0.6 0.0 copy-start.2
  0.7 0.0 copy-start.3
  0.7 0.0 copy-start.4
  0.7 53.3 %shard_map.129 = (bf16[256,2048]{1,0:T(8,128)(2,1)}, bf16[256,2048]{1,0:T(8,128)(2,1)}, bf16[4,512,256]{2,1,0:T(8,128)(2,1)}) custom-call(bf16[256,2048]{1,0:T(8,128)(2,1)} %bitcast.19, bf16[256,2048]{1,0:T(8,128)(2,1)} %bitcast.20, bf16[256,2048]{1,0:T(8,128)(2,1)} %bitcast.21, bf16[256,2048]{1,0:T(8,128)(2,1)} %bitcast.22, bf16[2048,256]{1,0:T(8,128)(2,1)} %filt_h.1, ...), custom_call_target="tpu_custom_call" | custom-call | flops 50331648 | bytes 12582912 | tf_op jit(solution)/shard_map/pallas_call | solution.py:376
  54.0 0.0 copy-start
  54.0 2.3 %convert_reduce_fusion = f32[512,256]{1,0:T(8,128)} fusion(bf16[4,512,256]{2,1,0:T(8,128)(2,1)} %get-tuple-element.9), kind=kLoop, calls=%fused_computation.10 | loop fusion | flops 917504 | bytes 1572864 | tf_op jit(solution)/shard_map/reduce_sum | solution.py:416
  56.3 0.0 copy-done.1
  56.3 0.0 copy-done.2
  56.3 0.0 copy-done.3
  56.3 0.0 copy-done.4
  56.3 0.0 copy-done
  56.3 4.6 %fusion.5 = (bf16[1,256,2048]{2,1,0:T(8,128)(2,1)}, bf16[1,256,2048]{2,1,0:T(8,128)(2,1)}, bf16[1,256,2048]{2,1,0:T(8,128)(2,1)}) fusion(bf16[256,2048]{1,0:T(8,128)(2,1)} %get-tuple-element.7, f32[2048]{0:T(1024)S(1)} %copy-done.4, bf16[1,256,2048]{2,1,0:T(8,128)(2,1)S(1)} %copy-done.3, bf16[1,256,2048]{2,1,0:T(8,128)(2,1)S(1)} %copy-done.2, ...), kind=kLoop, calls=%fused_computation.12 | loop fusion | flops 11534336 | bytes 9445376 | tf_op jit(solution)/shard_map/broadcast_in_dim | solution.py:417
Async XLA Ops:
  0.6 55.7 %copy-start.1 = (bf16[1,256,2048]{2,1,0:T(8,128)(2,1)S(1)}, bf16[1,256,2048]{2,1,0:T(8,128)(2,1)}, u32[]{:S(2)}) copy-start(bf16[1,256,2048]{2,1,0:T(8,128)(2,1)} %param.11) | copy-start | bytes 3145732
  0.6 55.7 %copy-start.2 = (bf16[1,256,2048]{2,1,0:T(8,128)(2,1)S(1)}, bf16[1,256,2048]{2,1,0:T(8,128)(2,1)}, u32[]{:S(2)}) copy-start(bf16[1,256,2048]{2,1,0:T(8,128)(2,1)} %param.12) | copy-start | bytes 3145732
  0.7 55.6 %copy-start.3 = (bf16[1,256,2048]{2,1,0:T(8,128)(2,1)S(1)}, bf16[1,256,2048]{2,1,0:T(8,128)(2,1)}, u32[]{:S(2)}) copy-start(bf16[1,256,2048]{2,1,0:T(8,128)(2,1)} %param.13) | copy-start | bytes 3145732
  0.7 55.6 %copy-start.4 = (f32[2048]{0:T(1024)S(1)}, f32[2048]{0:T(1024)}, u32[]{:S(2)}) copy-start(f32[2048]{0:T(1024)} %param.15) | copy-start | bytes 24580
  54.0 2.3 %copy-start = (bf16[1,256,2048]{2,1,0:T(8,128)(2,1)S(1)}, bf16[1,256,2048]{2,1,0:T(8,128)(2,1)}, u32[]{:S(2)}) copy-start(bf16[1,256,2048]{2,1,0:T(8,128)(2,1)} %param.10) | copy-start | bytes 3145732

commit v2 on v1

--- a/solution.py
+++ b/solution.py
@@ -115,9 +115,11 @@
     tb_h,
     tc_h,
     te_h,
-    conv_out,
-    back_out,
-    part_out,
+    gain_h,
+    in_out,
+    val_out,
+    gate_out,
+    filt_out,
     gin,
     val,
     gout,
@@ -127,10 +129,18 @@
     tb,
     tc,
     te,
+    gain,
     mid,
     spec_f,
     mixed,
     mixed_x,
+    conv_tok,
+    back_tok,
+    in_blk,
+    val_blk,
+    gate_blk,
+    parts,
+    filt_blk,
     *rest,
 ):
     me = lax.axis_index("ctx")
@@ -143,7 +153,7 @@
     groups = RADIX // GROUP
     piece = length // n_dp
     staged, landed, ret, own = (rest[i * halves : (i + 1) * halves] for i in range(4))
-    load_sem, own_sem, send_sem, recv_sem, dp_send, dp_recv = rest[4 * halves :]
+    first_sem, load_sem, own_sem, out_sem, send_sem, recv_sem, dp_send, dp_recv = rest[4 * halves :]
 
     barrier = pltpu.get_barrier_semaphore()
     for k in range(1, n_ctx):
@@ -151,24 +161,6 @@
     for k in range(1, n_dp):
         pl.semaphore_signal(barrier, inc=1, device_id={"dp": partner(seq, k, n_dp)})
 
-    loads = []
-    for i, (src, dst) in enumerate(
-        [
-            (gin_h, gin),
-            (val_h, val),
-            (cot_h, cot),
-            (gout_h, gout),
-            (filt_h, filt),
-            (ta_h, ta),
-            (tb_h, tb),
-            (tc_h, tc),
-            (te_h, te),
-        ]
-    ):
-        copy = pltpu.make_async_copy(src, dst, load_sem.at[i])
-        copy.start()
-        loads.append(copy)
-
     def span(start, count, unit):
         return pl.ds(pl.multiple_of(start, unit), count)
 
@@ -177,6 +169,23 @@
 
     def rows(index, count):
         return span(index * count, count, count)
+
+    def columns(index):
+        return span(index * chans, chans, chans)
+
+    order = send_order(n_ctx)
+
+    first_loads = {}
+    for k in order + [0]:
+        cols = columns(partner(me, k, n_ctx))
+        for i, (src, dst) in enumerate(((gin_h, gin), (val_h, val), (cot_h, cot), (gout_h, gout))):
+            copy = pltpu.make_async_copy(src.at[:, cols], dst.at[:, cols], first_sem.at[i, k])
+            copy.start()
+            first_loads[k, i] = copy
+
+    def wait_first(k):
+        for i in range(4):
+            first_loads[k, i].wait()
 
     def gate(h, index, target, where):
         cols = span(index * chans + h * lanes, lanes, lanes)
@@ -186,8 +195,10 @@
 
     def forward_sends(h):
         copies = []
-        for k in send_order(n_ctx):
+        for k in order:
             peer = partner(me, k, n_ctx)
+            if h == 0:
+                wait_first(k)
             gate(h, peer, staged[h], (slice(None), pair(peer)))
             copy = pltpu.make_async_remote_copy(
                 src_ref=staged[h].at[:, pair(peer)],
@@ -198,52 +209,85 @@
             )
             copy.start()
             copies.append(copy)
+        if h == 0:
+            wait_first(0)
         gate(h, me, landed[h], (rows(me, tok), slice(None)))
         return copies
 
     def return_sends(h):
-        copies = []
-        here = []
-        for t, target in enumerate((conv_out, back_out)):
-            dst = target.at[:, span(me * chans + h * lanes, lanes, lanes)]
-            cols = pl.ds(t * lanes, lanes)
-            for k in send_order(n_ctx):
-                peer = partner(me, k, n_ctx)
+        copies = {}
+        for k in order:
+            peer = partner(me, k, n_ctx)
+            for t, target in enumerate((conv_tok, back_tok)):
                 copy = pltpu.make_async_remote_copy(
-                    src_ref=ret[h].at[rows(peer, tok), cols],
-                    dst_ref=dst,
+                    src_ref=ret[h].at[rows(peer, tok), pl.ds(t * lanes, lanes)],
+                    dst_ref=target.at[:, span(me * chans + h * lanes, lanes, lanes)],
                     send_sem=send_sem.at[halves + 2 * h + t, k],
                     recv_sem=recv_sem.at[halves + 2 * h + t, k],
                     device_id={"ctx": peer},
                 )
                 copy.start()
-                copies.append(copy)
-            copy = pltpu.make_async_copy(
-                ret[h].at[rows(me, tok), cols], dst, own_sem.at[2 * h + t]
-            )
-            copy.start()
-            here.append(copy)
-        return copies, here
+                copies[k, t] = copy
+        return copies
 
     def part_sends(h):
         copies = []
-        cols = pl.ds(h * lanes, lanes)
         for k in range(1, n_dp):
             peer = partner(seq, k, n_dp)
             copy = pltpu.make_async_remote_copy(
                 src_ref=own[h].at[rows(peer, piece), :],
-                dst_ref=part_out.at[seq, :, cols],
+                dst_ref=parts.at[h, seq],
                 send_sem=dp_send.at[h, k],
                 recv_sem=dp_recv.at[h, k],
                 device_id={"dp": peer},
             )
             copy.start()
             copies.append(copy)
-        here = pltpu.make_async_copy(
-            own[h].at[rows(seq, piece), :], part_out.at[seq, :, cols], own_sem.at[2 * halves + h]
+        return copies
+
+    def finish_parts(h, copies):
+        for copy in copies:
+            copy.wait_recv()
+        total = own[h][rows(seq, piece), :].astype(F32)
+        for k in range(1, n_dp):
+            total = total + parts[h, partner(seq, k, n_dp)].astype(F32)
+        filt_blk[h] = total
+        copy = pltpu.make_async_copy(
+            filt_blk.at[h], filt_out.at[:, pl.ds(h * lanes, lanes)], own_sem.at[h]
         )
-        here.start()
-        return copies, [here]
+        copy.start()
+        return [copy]
+
+    def finish_block(h, k, conv, back):
+        cols = span(partner(me, k, n_ctx) * chans + h * lanes, lanes, lanes)
+        gain_row = gain[:, cols]
+        gin_f = gin[:, cols].astype(F32)
+        val_f = val[:, cols].astype(F32)
+        cot_f = cot[:, cols].astype(F32)
+        gated = (gin_f * val_f).astype(BF16).astype(F32)
+        grad = (cot_f * gout[:, cols].astype(F32)).astype(BF16).astype(F32)
+        gate_blk[:, cols] = (cot_f * (conv.astype(F32) + gain_row * gated)).astype(BF16)
+        grad_gated = back.astype(F32) + gain_row * grad
+        in_blk[:, cols] = (grad_gated * val_f).astype(BF16)
+        val_blk[:, cols] = (grad_gated * gin_f).astype(BF16)
+        copies = []
+        for i, (src, dst) in enumerate(
+            ((in_blk, in_out), (val_blk, val_out), (gate_blk, gate_out))
+        ):
+            copy = pltpu.make_async_copy(src.at[:, cols], dst.at[:, cols], out_sem.at[3 * h + i, k])
+            copy.start()
+            copies.append(copy)
+        return copies
+
+    def finish_blocks(h, copies):
+        block = ret[h][rows(me, tok), :]
+        done = finish_block(h, 0, block[:, :lanes], block[:, lanes:])
+        for k in order:
+            copies[k, 0].wait_recv()
+            copies[k, 1].wait_recv()
+            cols = span(partner(me, k, n_ctx) * chans + h * lanes, lanes, lanes)
+            done += finish_block(h, k, conv_tok[:, cols], back_tok[:, cols])
+        return done
 
     def repeat(first, count, most, step):
         width = max(w for w in range(1, most + 1) if count % w == 0)
@@ -324,39 +368,53 @@
         step(0, True)()
         repeat(1, half - 1, 5, lambda j: step(j, False))
 
-    for copy in loads[:4]:
-        copy.wait()
     pl.semaphore_wait(barrier, n_ctx - 1 + n_dp - 1)
     sent = [forward_sends(h) for h in range(halves)]
 
-    for copy in loads[4:]:
+    loads = []
+    for i, (src, dst) in enumerate(
+        [
+            (filt_h, filt),
+            (ta_h, ta),
+            (tb_h, tb),
+            (tc_h, tc),
+            (te_h, te),
+            (gain_h, gain),
+        ]
+    ):
+        copy = pltpu.make_async_copy(src, dst, load_sem.at[i])
+        copy.start()
+        loads.append(copy)
+    for copy in loads:
         copy.wait()
     first_stage(filt)
     each_row(filter_row)
 
-    remote = []
-    local = []
+    parted = []
+    returned = []
     for h in range(halves):
         for copy in sent[h]:
             copy.wait_recv()
         first_stage(landed[h])
         each_row(functools.partial(half_row, h))
         last_stage(mixed_x, own[h])
-        copies, here = part_sends(h)
-        remote += copies
-        local += here
+        parted.append(part_sends(h))
         last_stage(mixed, ret[h])
-        copies, here = return_sends(h)
-        remote += copies
-        local += here
-
-    for copy in sum(sent, []):
-        copy.wait_send()
-    for copy in local + remote:
+        returned.append(return_sends(h))
+
+    done = []
+    for h in range(halves):
+        done += finish_parts(h, parted[h])
+        done += finish_blocks(h, returned[h])
+
+    for h in range(halves):
+        for copy in sent[h] + parted[h] + list(returned[h].values()):
+            copy.wait_send()
+    for copy in done:
         copy.wait()
 
 
-def transfer_and_transform(gin, val, gout, cot, filters):
+def transfer_and_transform(gin, val, gout, cot, filters, gain):
     n_ctx = lax.axis_size("ctx")
     n_dp = lax.axis_size("dp")
     tok, width = gin.shape
@@ -366,54 +424,77 @@
     halves = max(1, chans // 128)
     lanes = chans // halves
     pair = 2 * lanes
-    outs = (
-        jax.ShapeDtypeStruct((tok, width), BF16),
-        jax.ShapeDtypeStruct((tok, width), BF16),
-        jax.ShapeDtypeStruct((n_dp, length // n_dp, chans), BF16),
+    piece = length // n_dp
+    outs = (jax.ShapeDtypeStruct((tok, width), BF16),) * 3 + (
+        jax.ShapeDtypeStruct((piece, chans), F32),
     )
     vmem = lambda *shape: pltpu.VMEM(shape, BF16)
     dma = lambda *shape: pltpu.SemaphoreType.DMA(shape)
     return pl.pallas_call(
         functools.partial(kernel, n_ctx, n_dp),
         out_shape=outs,
-        in_specs=[pl.BlockSpec(memory_space=pltpu.HBM)] * 9,
-        out_specs=[pl.BlockSpec(memory_space=pl.ANY)] * 3,
+        in_specs=[pl.BlockSpec(memory_space=pltpu.HBM)] * 10,
+        out_specs=[pl.BlockSpec(memory_space=pl.ANY)] * 4,
         scratch_shapes=[vmem(tok, width)] * 4
         + [vmem(length, chans)]
         + [vmem(*t.shape) for t in tables]
+        + [pltpu.VMEM((1, width), F32)]
         + [vmem(full, pair), vmem(full, chans), vmem(full, pair), vmem(full, lanes)]
+        + [vmem(tok, width)] * 5
+        + [vmem(halves, n_dp, piece, lanes), pltpu.VMEM((halves, piece, lanes), F32)]
         + [vmem(tok, n_ctx * pair)] * halves
         + [vmem(length, pair)] * halves
         + [vmem(length, pair)] * halves
         + [vmem(length, lanes)] * halves
-        + [dma(9), dma(3 * halves), dma(3 * halves, n_ctx), dma(3 * halves, n_ctx)]
+        + [dma(4, n_ctx), dma(6), dma(halves)]
+        + [dma(3 * halves, n_ctx)] * 3
         + [dma(halves, n_dp), dma(halves, n_dp)],
         compiler_params=pltpu.CompilerParams(
-            collective_id=0, has_side_effects=True, vmem_limit_bytes=56 * 2**20
+            collective_id=0, has_side_effects=True, vmem_limit_bytes=52 * 2**20
         ),
         cost_estimate=pl.CostEstimate(
             flops=12 * 2 * 512 * 256 * full * chans // 65536,
             bytes_accessed=12 * 2**20,
             transcendentals=0,
         ),
-    )(gin, val, gout, cot, filters, *tables)
+    )(gin, val, gout, cot, filters, *tables, gain)
+
+
+def publish_kernel(cuts, *refs):
+    count = len(refs) // 2
+    sems = refs[-1]
+    copies = []
+    for i in range(count):
+        src, dst = refs[i], refs[count + i]
+        size = src.shape[0] // cuts
+        for c in range(cuts):
+            where = pl.ds(c * size, size)
+            copy = pltpu.make_async_copy(src.at[where], dst.at[where], sems.at[i, c])
+            copy.start()
+            copies.append(copy)
+    for copy in copies:
+        copy.wait()
+
+
+def publish(results):
+    cuts = 4
+    any_spec = pl.BlockSpec(memory_space=pl.ANY)
+    size = sum(math.prod(r.shape) * r.dtype.itemsize for r in results)
+    return pl.pallas_call(
+        functools.partial(publish_kernel, cuts),
+        out_shape=tuple(jax.ShapeDtypeStruct(r.shape, r.dtype) for r in results),
+        in_specs=[any_spec] * len(results),
+        out_specs=[any_spec] * len(results),
+        scratch_shapes=[pltpu.SemaphoreType.DMA((len(results), cuts))],
+        cost_estimate=pl.CostEstimate(flops=0, bytes_accessed=2 * size, transcendentals=0),
+    )(*results)
 
 
 def on_device(gate_in, values, gate_out, cotangent, filters, skip_gain):
-    conv, back, parts = transfer_and_transform(
-        gate_in[0], values[0], gate_out[0], cotangent[0], filters
+    results = transfer_and_transform(
+        gate_in[0], values[0], gate_out[0], cotangent[0], filters, skip_gain[None, :]
     )
-    gin = gate_in[0].astype(F32)
-    vals = values[0].astype(F32)
-    cots = cotangent[0].astype(F32)
-    gated = (gin * vals).astype(BF16).astype(F32)
-    conv_grad = (cots * gate_out[0].astype(F32)).astype(BF16).astype(F32)
-    gain = skip_gain[None, :]
-    grad_gate_out = (cots * (conv.astype(F32) + gain * gated)).astype(BF16)
-    grad_gated = back.astype(F32) + gain * conv_grad
-    grad_gate_in = (grad_gated * vals).astype(BF16)
-    grad_values = (grad_gated * gin).astype(BF16)
-    grad_filters = jnp.sum(parts.astype(F32), axis=0)
+    grad_gate_in, grad_values, grad_gate_out, grad_filters = publish(results)
     return (grad_gate_in[None], grad_values[None], grad_gate_out[None], grad_filters)
 
 

time: 61.1 us -> 172 us (2.82)
  Pallas kernels: 53.3 us -> 167 us
  other arithmetic: 6.93 us -> 0 us
  local copies, waits for them, and re-layouts: 0.02 us -> 3.38 us
    pallas_call x0 -> x1, Pallas kernels: none -> 112 us  [publish(): pl.pallas_call(functools.partial(publish_kernel, cuts), out_shape=tuple((...]
    broadcast_in_dim x1 -> x0, other arithmetic: 4.64 us -> none  [on_device(): grad_values[None]]
    unnamed x10 -> x8, local copies, waits for them, and re-layouts: 0.02 us -> 3.38 us
    reduce_sum x1 -> x0, other arithmetic: 2.29 us -> none  [on_device(): grad_filters = jnp.sum(parts.astype(F32), axis=0)]
where the time goes in v2:
time: 172 us; the launch traced here: 171 us
  Pallas kernels  167 us (97%)
  local copies, waits for them, and re-layouts  3.38 us (2%)
    pallas_call x1, Pallas kernels, publish(): pl.pallas_call(functools.partial(publish_kernel, cuts), out_shape=tuple((...  112 us
    pallas_call x1, Pallas kernels, transfer_and_transform(): pl.pallas_call(functools.partial(kernel, n_ctx, n_dp), out_shape=outs, in...  54.8 us

profile of v2, /device:TPU:0, one launch (start us, length us, event | category | flops | bytes accessed | tf_op | source)
XLA Modules:
  0.0 171.3 jit_solution(17295830012515664916)
XLA Ops:
  0.6 0.0 copy-start.1
  0.6 0.9 copy-done.1
  1.6 0.0 copy-start.2
  1.6 0.9 copy-done.2
  2.5 0.0 copy-start.3
  2.5 0.7 copy-done.3
  3.2 54.8 %shard_map.129 = (bf16[256,2048]{1,0:T(8,128)(2,1)}, bf16[256,2048]{1,0:T(8,128)(2,1)}, bf16[256,2048]{1,0:T(8,128)(2,1)}, f32[512,256]{1,0:T(8,128)S(1)}) custom-call(bf16[256,2048]{1,0:T(8,128)(2,1)} %bitcast.9, bf16[256,2048]{1,0:T(8,128)(2,1)} %bitcast.10, bf16[256,2048]{1,0:T(8,128)(2,1)} %bitcast.11, bf16[256,2048]{1,0:T(8,128)(2,1)} %bitcast.12, ...), custom_call_target="tpu_custom_call" | custom-call | flops 50331648 | bytes 12582912 | tf_op jit(solution)/shard_map/pallas_call | solution.py:433
  58.1 0.0 copy-start
  58.1 0.8 copy-done
  58.9 112.4 %shard_map.130 = (bf16[256,2048]{1,0:T(8,128)(2,1)}, bf16[256,2048]{1,0:T(8,128)(2,1)}, bf16[256,2048]{1,0:T(8,128)(2,1)}, f32[512,256]{1,0:T(8,128)}) custom-call(bf16[256,2048]{1,0:T(8,128)(2,1)} %get-tuple-element.12.refs_0_, bf16[256,2048]{1,0:T(8,128)(2,1)} %get-tuple-element.13.refs_1_, bf16[256,2048]{1,0:T(8,128)(2,1)} %get-tuple-element.14.refs_2_, ...), custom_call_target="tpu_custom_call" | custom-call | bytes 7340032 | tf_op jit(solution)/shard_map/pallas_call | solution.py:483
Async XLA Ops:
  0.6 1.0 copy-start.1
  1.6 0.9 copy-start.2
  2.5 0.7 copy-start.3
  58.1 0.8 copy-start

commit v3 on v2

--- a/solution.py
+++ b/solution.py
@@ -58,9 +58,14 @@
     packed_inv[0, :, 0, 0] = 1.0
     packed_inv[0, :, 1, 0] = (-1.0) ** b
     full = 2 * RADIX
-    table_b = np.stack([packed.reshape(full, full), general])
-    table_c = np.stack([packed_inv.reshape(full, full), inverse])
-    return tuple(t.astype(ml_dtypes.bfloat16) for t in (table_a, table_b, table_c, table_e))
+    table_b = np.concatenate([packed.reshape(full, full), general], 1)
+    table_c = np.concatenate([packed_inv.reshape(full, full), inverse], 1)
+    wide = table_e.shape[2]
+    joined = np.concatenate(
+        [np.pad(t, ((0, 0), (0, wide - 2 * full))) for t in (table_b, table_c)]
+        + [table_e.reshape(-1, wide)]
+    )
+    return tuple(t.astype(ml_dtypes.bfloat16) for t in (table_a, joined))
 
 
 def dot(left, right):
@@ -112,8 +117,6 @@
     cot_h,
     filt_h,
     ta_h,
-    tb_h,
-    tc_h,
     te_h,
     gain_h,
     in_out,
@@ -126,8 +129,6 @@
     cot,
     filt,
     ta,
-    tb,
-    tc,
     te,
     gain,
     mid,
@@ -136,11 +137,7 @@
     mixed_x,
     conv_tok,
     back_tok,
-    in_blk,
-    val_blk,
-    gate_blk,
     parts,
-    filt_blk,
     *rest,
 ):
     me = lax.axis_index("ctx")
@@ -153,7 +150,7 @@
     groups = RADIX // GROUP
     piece = length // n_dp
     staged, landed, ret, own = (rest[i * halves : (i + 1) * halves] for i in range(4))
-    first_sem, load_sem, own_sem, out_sem, send_sem, recv_sem, dp_send, dp_recv = rest[4 * halves :]
+    first_sem, load_sem, send_sem, recv_sem, dp_send, dp_recv = rest[4 * halves :]
 
     barrier = pltpu.get_barrier_semaphore()
     for k in range(1, n_ctx):
@@ -251,12 +248,7 @@
         total = own[h][rows(seq, piece), :].astype(F32)
         for k in range(1, n_dp):
             total = total + parts[h, partner(seq, k, n_dp)].astype(F32)
-        filt_blk[h] = total
-        copy = pltpu.make_async_copy(
-            filt_blk.at[h], filt_out.at[:, pl.ds(h * lanes, lanes)], own_sem.at[h]
-        )
-        copy.start()
-        return [copy]
+        filt_out[:, h * lanes : (h + 1) * lanes] = total
 
     def finish_block(h, k, conv, back):
         cols = span(partner(me, k, n_ctx) * chans + h * lanes, lanes, lanes)
@@ -266,28 +258,19 @@
         cot_f = cot[:, cols].astype(F32)
         gated = (gin_f * val_f).astype(BF16).astype(F32)
         grad = (cot_f * gout[:, cols].astype(F32)).astype(BF16).astype(F32)
-        gate_blk[:, cols] = (cot_f * (conv.astype(F32) + gain_row * gated)).astype(BF16)
+        gate_out[:, cols] = (cot_f * (conv.astype(F32) + gain_row * gated)).astype(BF16)
         grad_gated = back.astype(F32) + gain_row * grad
-        in_blk[:, cols] = (grad_gated * val_f).astype(BF16)
-        val_blk[:, cols] = (grad_gated * gin_f).astype(BF16)
-        copies = []
-        for i, (src, dst) in enumerate(
-            ((in_blk, in_out), (val_blk, val_out), (gate_blk, gate_out))
-        ):
-            copy = pltpu.make_async_copy(src.at[:, cols], dst.at[:, cols], out_sem.at[3 * h + i, k])
-            copy.start()
-            copies.append(copy)
-        return copies
+        in_out[:, cols] = (grad_gated * val_f).astype(BF16)
+        val_out[:, cols] = (grad_gated * gin_f).astype(BF16)
 
     def finish_blocks(h, copies):
         block = ret[h][rows(me, tok), :]
-        done = finish_block(h, 0, block[:, :lanes], block[:, lanes:])
+        finish_block(h, 0, block[:, :lanes], block[:, lanes:])
         for k in order:
             copies[k, 0].wait_recv()
             copies[k, 1].wait_recv()
             cols = span(partner(me, k, n_ctx) * chans + h * lanes, lanes, lanes)
-            done += finish_block(h, k, conv_tok[:, cols], back_tok[:, cols])
-        return done
+            finish_block(h, k, conv_tok[:, cols], back_tok[:, cols])
 
     def repeat(first, count, most, step):
         width = max(w for w in range(1, most + 1) if count % w == 0)
@@ -320,7 +303,7 @@
             part = [
                 source[span(row * RADIX + g * GROUP, GROUP, GROUP), :] for row in range(2 * half)
             ]
-            out = dot(te[g], jnp.concatenate(part, 0)).astype(BF16)
+            out = dot(te[span(4 * RADIX + g * half * GROUP, half * GROUP, GROUP), :], jnp.concatenate(part, 0)).astype(BF16)
 
             def store():
                 for a in range(half):
@@ -332,9 +315,13 @@
 
         repeat(0, groups, 4, step)
 
+    def second(which, packed):
+        col = 0 if packed else 2 * RADIX
+        return te[pl.ds(which * 2 * RADIX, 2 * RADIX), pl.ds(col, 2 * RADIX)]
+
     def filter_row(j, packed):
         where = rows(j, 2 * RADIX)
-        spec = dot(tb[0 if packed else 1], mid[where, :chans]).astype(BF16)
+        spec = dot(second(0, packed), mid[where, :chans]).astype(BF16)
 
         def store():
             spec_f[where, :] = spec
@@ -343,8 +330,7 @@
 
     def half_row(h, j, packed):
         where = rows(j, 2 * RADIX)
-        which = 0 if packed else 1
-        spec = dot(tb[which], mid[where, :]).astype(BF16)
+        spec = dot(second(0, packed), mid[where, :]).astype(BF16)
         spec_g, spec_c = spec[:, :lanes], spec[:, lanes:]
         filt_row = spec_f[where, h * lanes : (h + 1) * lanes]
         cross = spectral_product(spec_g, spec_c, True, packed)
@@ -355,8 +341,8 @@
             ],
             1,
         )
-        out_x = dot(tc[which], cross).astype(BF16)
-        out = dot(tc[which], both).astype(BF16)
+        out_x = dot(second(1, packed), cross).astype(BF16)
+        out = dot(second(1, packed), both).astype(BF16)
 
         def store():
             mixed_x[where, :] = out_x
@@ -376,8 +362,6 @@
         [
             (filt_h, filt),
             (ta_h, ta),
-            (tb_h, tb),
-            (tc_h, tc),
             (te_h, te),
             (gain_h, gain),
         ]
@@ -397,21 +381,22 @@
             copy.wait_recv()
         first_stage(landed[h])
         each_row(functools.partial(half_row, h))
-        last_stage(mixed_x, own[h])
-        parted.append(part_sends(h))
+        if h == halves - 1:
+            last_stage(mixed_x, own[h])
+            parted.append(part_sends(h))
         last_stage(mixed, ret[h])
         returned.append(return_sends(h))
-
-    done = []
+        if h < halves - 1:
+            last_stage(mixed_x, own[h])
+            parted.append(part_sends(h))
+
     for h in range(halves):
-        done += finish_parts(h, parted[h])
-        done += finish_blocks(h, returned[h])
+        finish_parts(h, parted[h])
+        finish_blocks(h, returned[h])
 
     for h in range(halves):
         for copy in sent[h] + parted[h] + list(returned[h].values()):
             copy.wait_send()
-    for copy in done:
-        copy.wait()
 
 
 def transfer_and_transform(gin, val, gout, cot, filters, gain):
@@ -425,32 +410,30 @@
     lanes = chans // halves
     pair = 2 * lanes
     piece = length // n_dp
-    outs = (jax.ShapeDtypeStruct((tok, width), BF16),) * 3 + (
-        jax.ShapeDtypeStruct((piece, chans), F32),
-    )
+    outs = (pltpu.VMEM((tok, width), BF16),) * 3 + (pltpu.VMEM((piece, chans), F32),)
     vmem = lambda *shape: pltpu.VMEM(shape, BF16)
     dma = lambda *shape: pltpu.SemaphoreType.DMA(shape)
     return pl.pallas_call(
         functools.partial(kernel, n_ctx, n_dp),
         out_shape=outs,
-        in_specs=[pl.BlockSpec(memory_space=pltpu.HBM)] * 10,
-        out_specs=[pl.BlockSpec(memory_space=pl.ANY)] * 4,
+        in_specs=[pl.BlockSpec(memory_space=pltpu.HBM)] * 8,
+        out_specs=[pl.BlockSpec(memory_space=pltpu.VMEM)] * 4,
         scratch_shapes=[vmem(tok, width)] * 4
         + [vmem(length, chans)]
         + [vmem(*t.shape) for t in tables]
         + [pltpu.VMEM((1, width), F32)]
         + [vmem(full, pair), vmem(full, chans), vmem(full, pair), vmem(full, lanes)]
-        + [vmem(tok, width)] * 5
-        + [vmem(halves, n_dp, piece, lanes), pltpu.VMEM((halves, piece, lanes), F32)]
+        + [vmem(tok, width)] * 2
+        + [vmem(halves, n_dp, piece, lanes)]
         + [vmem(tok, n_ctx * pair)] * halves
         + [vmem(length, pair)] * halves
         + [vmem(length, pair)] * halves
         + [vmem(length, lanes)] * halves
-        + [dma(4, n_ctx), dma(6), dma(halves)]
-        + [dma(3 * halves, n_ctx)] * 3
+        + [dma(4, n_ctx), dma(4)]
+        + [dma(3 * halves, n_ctx)] * 2
         + [dma(halves, n_dp), dma(halves, n_dp)],
         compiler_params=pltpu.CompilerParams(
-            collective_id=0, has_side_effects=True, vmem_limit_bytes=52 * 2**20
+            collective_id=0, has_side_effects=True, vmem_limit_bytes=56 * 2**20
         ),
         cost_estimate=pl.CostEstimate(
             flops=12 * 2 * 512 * 256 * full * chans // 65536,
@@ -483,7 +466,7 @@
     return pl.pallas_call(
         functools.partial(publish_kernel, cuts),
         out_shape=tuple(jax.ShapeDtypeStruct(r.shape, r.dtype) for r in results),
-        in_specs=[any_spec] * len(results),
+        in_specs=[pl.BlockSpec(memory_space=pltpu.VMEM)] * len(results),
         out_specs=[any_spec] * len(results),
         scratch_shapes=[pltpu.SemaphoreType.DMA((len(results), cuts))],
         cost_estimate=pl.CostEstimate(flops=0, bytes_accessed=2 * size, transcendentals=0),

time: 172 us -> 62.4 us (0.36)
  Pallas kernels: 167 us -> 57.8 us
    pallas_call x1, Pallas kernels: 112 us -> 3.94 us  [publish(): pl.pallas_call(functools.partial(publish_kernel, cuts), out_shape=tuple((...]
where the time goes in v3:
time: 62.4 us; the launch traced here: 62.2 us
  Pallas kernels  57.8 us (93%)
  local copies, waits for them, and re-layouts  3.77 us (6%)
  between operations  0.65 us (1%)
    pallas_call x1, Pallas kernels, transfer_and_transform(): pl.pallas_call(functools.partial(kernel, n_ctx, n_dp), out_shape=outs, in...  53.9 us
    pallas_call x1, Pallas kernels, publish(): pl.pallas_call(functools.partial(publish_kernel, cuts), out_shape=tuple((...  3.94 us
    unnamed x8, local copies, waits for them, and re-layouts  3.77 us

profile of v3, /device:TPU:0, one launch (start us, length us, event | category | flops | bytes accessed | tf_op | source)
XLA Modules:
  0.0 62.2 jit_solution(18436663664217169904)
XLA Ops:
  0.6 53.9 %shard_map.111 = (bf16[256,2048]{1,0:T(8,128)(2,1)S(1)}, bf16[256,2048]{1,0:T(8,128)(2,1)S(1)}, bf16[256,2048]{1,0:T(8,128)(2,1)S(1)}, f32[512,256]{1,0:T(8,128)S(1)}) custom-call(bf16[256,2048]{1,0:T(8,128)(2,1)} %bitcast.8, bf16[256,2048]{1,0:T(8,128)(2,1)} %bitcast.9, bf16[256,2048]{1,0:T(8,128)(2,1)} %bitcast.10, bf16[256,2048]{1,0:T(8,128)(2,1)} %bitcast.11, ...), custom_call_target="tpu_custom_call" | custom-call | flops 50331648 | bytes 12582912 | tf_op jit(solution)/shard_map/pallas_call | solution.py:416
  54.5 0.0 copy-start
  54.5 1.0 %copy-done = bf16[256,2048]{1,0:T(8,128)(2,1)} copy-done((bf16[256,2048]{1,0:T(8,128)(2,1)}, bf16[256,2048]{1,0:T(8,128)(2,1)S(1)}, u32[]{:S(2)}) %copy-start) | copy-done | bytes 1048600
  55.5 0.0 copy-start.1
  55.5 1.0 %copy-done.1 = bf16[256,2048]{1,0:T(8,128)(2,1)} copy-done((bf16[256,2048]{1,0:T(8,128)(2,1)}, bf16[256,2048]{1,0:T(8,128)(2,1)S(1)}, u32[]{:S(2)}) %copy-start.1) | copy-done | bytes 1048600
  56.5 0.0 copy-start.2
  56.5 1.0 %copy-done.2 = bf16[256,2048]{1,0:T(8,128)(2,1)} copy-done((bf16[256,2048]{1,0:T(8,128)(2,1)}, bf16[256,2048]{1,0:T(8,128)(2,1)S(1)}, u32[]{:S(2)}) %copy-start.2) | copy-done | bytes 1048600
  57.5 0.0 copy-start.3
  57.5 0.8 %copy-done.3 = f32[512,256]{1,0:T(8,128)} copy-done((f32[512,256]{1,0:T(8,128)}, f32[512,256]{1,0:T(8,128)S(1)}, u32[]{:S(2)}) %copy-start.3) | copy-done | bytes 524312
  58.3 3.9 %shard_map.112 = (bf16[256,2048]{1,0:T(8,128)(2,1)}, bf16[256,2048]{1,0:T(8,128)(2,1)}, bf16[256,2048]{1,0:T(8,128)(2,1)}, f32[512,256]{1,0:T(8,128)}) custom-call(bf16[256,2048]{1,0:T(8,128)(2,1)} %copy-done, bf16[256,2048]{1,0:T(8,128)(2,1)} %copy-done.1, bf16[256,2048]{1,0:T(8,128)(2,1)} %copy-done.2, f32[512,256]{1,0:T(8,128)} %copy-done.3), custom_call_target="tpu_custom_call" | custom-call | bytes 7340032 | tf_op jit(solution)/shard_map/pallas_call | solution.py:466
Async XLA Ops:
  54.5 1.0 %copy-start = (bf16[256,2048]{1,0:T(8,128)(2,1)}, bf16[256,2048]{1,0:T(8,128)(2,1)S(1)}, u32[]{:S(2)}) copy-start(bf16[256,2048]{1,0:T(8,128)(2,1)S(1)} %get-tuple-element.12.refs_0_) | copy-start | bytes 3145732
  55.5 1.0 %copy-start.1 = (bf16[256,2048]{1,0:T(8,128)(2,1)}, bf16[256,2048]{1,0:T(8,128)(2,1)S(1)}, u32[]{:S(2)}) copy-start(bf16[256,2048]{1,0:T(8,128)(2,1)S(1)} %get-tuple-element.13.refs_1_) | copy-start | bytes 3145732
  56.5 1.0 %copy-start.2 = (bf16[256,2048]{1,0:T(8,128)(2,1)}, bf16[256,2048]{1,0:T(8,128)(2,1)S(1)}, u32[]{:S(2)}) copy-start(bf16[256,2048]{1,0:T(8,128)(2,1)S(1)} %get-tuple-element.14.refs_2_) | copy-start | bytes 3145732
  57.5 0.8 %copy-start.3 = (f32[512,256]{1,0:T(8,128)}, f32[512,256]{1,0:T(8,128)S(1)}, u32[]{:S(2)}) copy-start(f32[512,256]{1,0:T(8,128)S(1)} %get-tuple-element.15.refs_3_) | copy-start | bytes 1572868

commit v4 on v3

--- a/solution.py
+++ b/solution.py
@@ -443,41 +443,10 @@
     )(gin, val, gout, cot, filters, *tables, gain)
 
 
-def publish_kernel(cuts, *refs):
-    count = len(refs) // 2
-    sems = refs[-1]
-    copies = []
-    for i in range(count):
-        src, dst = refs[i], refs[count + i]
-        size = src.shape[0] // cuts
-        for c in range(cuts):
-            where = pl.ds(c * size, size)
-            copy = pltpu.make_async_copy(src.at[where], dst.at[where], sems.at[i, c])
-            copy.start()
-            copies.append(copy)
-    for copy in copies:
-        copy.wait()
-
-
-def publish(results):
-    cuts = 4
-    any_spec = pl.BlockSpec(memory_space=pl.ANY)
-    size = sum(math.prod(r.shape) * r.dtype.itemsize for r in results)
-    return pl.pallas_call(
-        functools.partial(publish_kernel, cuts),
-        out_shape=tuple(jax.ShapeDtypeStruct(r.shape, r.dtype) for r in results),
-        in_specs=[pl.BlockSpec(memory_space=pltpu.VMEM)] * len(results),
-        out_specs=[any_spec] * len(results),
-        scratch_shapes=[pltpu.SemaphoreType.DMA((len(results), cuts))],
-        cost_estimate=pl.CostEstimate(flops=0, bytes_accessed=2 * size, transcendentals=0),
-    )(*results)
-
-
 def on_device(gate_in, values, gate_out, cotangent, filters, skip_gain):
-    results = transfer_and_transform(
+    grad_gate_in, grad_values, grad_gate_out, grad_filters = transfer_and_transform(
         gate_in[0], values[0], gate_out[0], cotangent[0], filters, skip_gain[None, :]
     )
-    grad_gate_in, grad_values, grad_gate_out, grad_filters = publish(results)
     return (grad_gate_in[None], grad_values[None], grad_gate_out[None], grad_filters)
 
 

time: 62.4 us -> 58.4 us (0.936)
  Pallas kernels: 57.8 us -> 53.9 us
    pallas_call x1 -> x0, Pallas kernels: 3.94 us -> none  [publish(): pl.pallas_call(functools.partial(publish_kernel, cuts), out_shape=tuple((...]
    unnamed x8 -> x4, local copies, waits for them, and re-layouts: 3.77 us -> 3.7 us
where the time goes in v4:
time: 58.4 us; the launch traced here: 58.2 us
  Pallas kernels  53.9 us (92%)
  local copies, waits for them, and re-layouts  3.7 us (6%)
  between operations  0.64 us (1%)
    pallas_call x1, Pallas kernels, transfer_and_transform(): pl.pallas_call(functools.partial(kernel, n_ctx, n_dp), out_shape=outs, in...  53.9 us
    unnamed x4, local copies, waits for them, and re-layouts  3.7 us

profile of v4, /device:TPU:0, one launch (start us, length us, event | category | flops | bytes accessed | tf_op | source)
XLA Modules:
  0.0 58.2 jit_solution(16625103901369197403)
XLA Ops:
  0.6 53.9 %shard_map.111 = (bf16[256,2048]{1,0:T(8,128)(2,1)S(1)}, bf16[256,2048]{1,0:T(8,128)(2,1)S(1)}, bf16[256,2048]{1,0:T(8,128)(2,1)S(1)}, f32[512,256]{1,0:T(8,128)S(1)}) custom-call(bf16[256,2048]{1,0:T(8,128)(2,1)} %bitcast.11, bf16[256,2048]{1,0:T(8,128)(2,1)} %bitcast.12, bf16[256,2048]{1,0:T(8,128)(2,1)} %bitcast.13, bf16[256,2048]{1,0:T(8,128)(2,1)} %bitcast.14, ...), custom_call_target="tpu_custom_call" | custom-call | flops 50331648 | bytes 12582912 | tf_op jit(solution)/shard_map/pallas_call | solution.py:416
  54.5 1.0 %copy.16 = bf16[1,256,2048]{2,1,0:T(8,128)(2,1)} copy(bf16[1,256,2048]{2,1,0:T(8,128)(2,1)S(1)} %bitcast.10) | data formatting | bytes 2097152
  55.5 1.0 %copy.17 = bf16[1,256,2048]{2,1,0:T(8,128)(2,1)} copy(bf16[1,256,2048]{2,1,0:T(8,128)(2,1)S(1)} %bitcast.9) | data formatting | bytes 2097152
  56.5 0.8 %copy.19 = f32[512,256]{1,0:T(8,128)} copy(f32[512,256]{1,0:T(8,128)S(1)} %get-tuple-element.15) | data formatting | bytes 1048576
  57.3 1.0 %copy.18 = bf16[1,256,2048]{2,1,0:T(8,128)(2,1)} copy(bf16[1,256,2048]{2,1,0:T(8,128)(2,1)S(1)} %bitcast.8) | data formatting | bytes 2097152
